TPU v7x, 256 devices: a whole 4x4x8 slice. The times are simulated.
256 devices in a mesh: fsdp: 32 (over y, x, core), ctx: 8 (over z).
Axes of the slice: x: 4, y: 4, z: 8, core: 2. Of those that a mesh axis runs over, the one named last changes fastest.
Arguments:
- tokens: bfloat16 [16384, 8192], P('fsdp'), may hold values from -12 to 12
- wq: bfloat16 [8192, 4096], P('fsdp', 'ctx'), may hold values from -0.0625 to 0.0625
- wo: bfloat16 [4096, 8192], P('ctx', 'fsdp'), may hold values from -1.5 to 1.5
- key_cache: bfloat16 [65536, 1024], P(('fsdp', 'ctx')), may hold values from -500 to 500, as said below
- value_cache: bfloat16 [65536, 1024], P(('fsdp', 'ctx')), may hold values from -6 to 6
- key_blocks: int32 [32, 4, 8], P('fsdp'), may hold values from 0 to 15, as said below
Outputs:
- mixed: bfloat16 [16384, 8192], P('fsdp', 'ctx')
Inputs may be any that keep to these rules, and one draw needn't show every extreme that they name: `key_cache`: keys of order one; a sequence's first block may hold much larger ones. `key_blocks`: for query block b of sequence s, entries 0 to 2 name key blocks 16 - 4 + b - 2, 12 + b - 1 and 12 + b; entries 3 and 4 name blocks 0 and 1; the last 3 entries are random blocks. Counting the random entries of a sequence over its query blocks in order as t = 0, 1, ..., the t-th lies in blocks k * 2 to (k+1) * 2 - 1 with k = 1 + t mod (6); entries may repeat.
All inputs are finite; a program needn't handle non-finite values.
Results may differ from a plain program's by a relative error of at most 0.018.
Values may be sent and summed in bfloat16 or wider, within the bound.
No kernel may reach another device: no remote copies, remote signals or barrier semaphores. Data moves between devices by JAX's collectives and lax.ppermute only.
A program may use at most 128 MiB of HBM per device.

v0:
```python
import jax
import jax.numpy as jnp
from jax import lax
from jax.sharding import PartitionSpec as P

HEAD = 128
BLOCK = 128
rope_base = 1000000.0


def rotate(vectors, positions):
    half_width = vectors.shape[-1] // 2
    frequency = rope_base ** (
        -(jnp.arange(half_width, dtype=jnp.float32) * 2.0) / vectors.shape[-1]
    )
    angles = positions.astype(jnp.float32)[:, None] * frequency[None, :]
    cosine_table = jnp.cos(angles)[:, None, :]
    sine_table = jnp.sin(angles)[:, None, :]
    front_half = vectors[..., :half_width]
    back_half = vectors[..., half_width:]
    return jnp.concatenate(
        [
            front_half * cosine_table - back_half * sine_table,
            back_half * cosine_table + front_half * sine_table,
        ],
        axis=-1,
    )


def body(tokens, wq, wo, key_cache, value_cache, key_blocks):
    ctx_count = lax.axis_size("ctx")
    row_count = tokens.shape[0]
    query_cols = wq.shape[1]
    projected = jnp.dot(
        tokens, lax.all_gather(wq, "fsdp", axis=0, tiled=True), preferred_element_type=jnp.float32
    )
    cache_count = key_cache.shape[0]
    key_total = cache_count * ctx_count
    positions = key_total - row_count + jnp.arange(row_count, dtype=jnp.int32)
    query = (
        rotate(projected.reshape(row_count, query_cols // HEAD, HEAD), positions) * HEAD ** (-0.5)
    ).astype(jnp.bfloat16)
    kv_cols = key_cache.shape[1] // ctx_count
    keys_whole, values_whole = (
        lax.all_gather(key_cache, "ctx", axis=0, tiled=True),
        lax.all_gather(value_cache, "ctx", axis=0, tiled=True),
    )
    first_col = lax.axis_index("ctx") * kv_cols
    keys_all = lax.dynamic_slice_in_dim(keys_whole, first_col, kv_cols, 1)
    values_all = lax.dynamic_slice_in_dim(values_whole, first_col, kv_cols, 1)
    kv_local = kv_cols // HEAD
    group_size = query_cols // kv_cols
    block_count = key_total // BLOCK
    query_blocks = row_count // BLOCK
    lists = key_blocks[0]
    picked_keys = jnp.take(keys_all.reshape(block_count, BLOCK, kv_local, HEAD), lists, axis=0)
    picked_values = jnp.take(values_all.reshape(block_count, BLOCK, kv_local, HEAD), lists, axis=0)
    shaped = query.reshape(query_blocks, BLOCK, kv_local, group_size, HEAD)
    scores = jnp.einsum(
        "bqkgd,bnskd->bkgqns", shaped, picked_keys, preferred_element_type=jnp.float32
    )
    own_block = block_count - query_blocks + jnp.arange(query_blocks, dtype=jnp.int32)
    own = lists == own_block[:, None]
    causal = jnp.arange(BLOCK)[None, :] <= jnp.arange(BLOCK)[:, None]
    allowed = jnp.logical_or(
        jnp.logical_not(own)[:, None, None, None, :, None], causal[None, None, None, :, None, :]
    )
    scores = jnp.where(allowed, scores, -jnp.inf)
    top_score = jnp.max(scores, axis=(4, 5), keepdims=True)
    raised = jnp.exp(scores - top_score)
    weights = (raised / jnp.sum(raised, axis=(4, 5), keepdims=True)).astype(jnp.bfloat16)
    context = jnp.einsum(
        "bkgqns,bnskd->bqkgd", weights, picked_values, preferred_element_type=jnp.float32
    )
    context = context.astype(jnp.bfloat16).reshape(row_count, query_cols)
    share_terms = jnp.dot(
        context, lax.all_gather(wo, "fsdp", axis=1, tiled=True), preferred_element_type=jnp.float32
    )
    return lax.psum_scatter(
        share_terms.astype(jnp.bfloat16), "ctx", scatter_dimension=1, tiled=True
    )


def solution(mesh):
    in_specs = (
        P("fsdp", None),
        P("fsdp", "ctx"),
        P("ctx", "fsdp"),
        P(("fsdp", "ctx"), None),
        P(("fsdp", "ctx"), None),
        P("fsdp", None, None),
    )
    out_specs = P("fsdp", "ctx")
    return jax.shard_map(body, mesh=mesh, in_specs=in_specs, out_specs=out_specs, check_vma=False)
```

profile of v0, /device:TPU:1, one launch (start us, length us, event | category | flops | bytes accessed | tf_op | source)
XLA Modules:
  0.0 360.2 jit_solution(5195303256417563035)
XLA Ops:
  6.5 0.0 all-gather.5.cloned.1.call-start
  6.5 0.7 all-gather.5.cloned.1.call-update
  7.3 0.0 all-gather.7.cloned.1.call-start
  7.3 0.7 all-gather.7.cloned.1.call-update
  8.0 0.0 all-gather.9.cloned.1.call-start
  8.1 0.7 all-gather.9.cloned.1.call-update
  8.7 0.0 all-gather.11.cloned.1.call-start
  8.8 0.5 all-gather.11.cloned.1.call-update
  9.3 0.0 reduce-scatter.2.cloned.1.call-start
  9.4 0.7 compare_select_fusion
  10.1 0.1 reshape.192
  10.2 0.8 fusion.28
  11.0 0.5 multiply_cosine_fusion
  11.5 0.3 broadcast_or_fusion
  11.8 56.0 %all-gather.5.cloned.1.call-done = bf16[2048,1024]{1,0:T(8,128)(2,1)} async-done(((bf16[256,1024]{1,0:T(8,128)(2,1)}), bf16[2048,1024]{1,0:T(8,128)(2,1)}) %all-gather.5.cloned.1.call-update) | async-done | bytes 4194320 | tf_op jit(solution)/shard_map/all_gather | solution.py:46
  67.8 55.2 %all-gather.7.cloned.1.call-done = bf16[2048,1024]{1,0:T(8,128)(2,1)} async-done(((bf16[256,1024]{1,0:T(8,128)(2,1)}), bf16[2048,1024]{1,0:T(8,128)(2,1)}) %all-gather.7.cloned.1.call-update) | async-done | bytes 4194320 | tf_op jit(solution)/shard_map/all_gather | solution.py:45
  123.0 1.3 constant_dynamic-slice_fusion
  124.3 0.7 gather_fusion.1
  125.1 0.7 gather_fusion
  125.8 1.3 copy.8
  127.2 55.4 %all-gather.9.cloned.1.call-done = bf16[8192,512]{1,0:T(8,128)(2,1)} async-done(((bf16[256,512]{1,0:T(8,128)(2,1)}), bf16[8192,512]{1,0:T(8,128)(2,1)}) %all-gather.9.cloned.1.call-update) | async-done | bytes 8388624 | tf_op jit(solution)/shard_map/all_gather | solution.py:35
  182.6 9.4 %fusion.34 = f32[512,512]{0,1:T(8,128)S(1)} fusion(bf16[512,8192]{1,0:T(8,128)(2,1)} %param.8, bf16[8192,512]{1,0:T(8,128)(2,1)} %all-gather.9.cloned.1.call-done), kind=kOutput, calls=%fused_computation.49 | convolution fusion | flops 4294967296 | bytes 17825792 | tf_op jit(solution)/shard_map/dot_general | solution.py:34
  192.0 1.0 multiply_subtract_fusion
  193.0 0.2 concatenate.10
  193.2 0.3 copy.10
  193.5 1.2 concatenate.9
  194.7 1.3 copy.9
  196.0 2.7 fusion
  198.7 0.0 copy-start
  198.7 1.7 fusion.1
  200.5 0.0 copy-done
  200.5 2.2 fusion.10
  202.7 0.3 copy.12
  203.0 46.1 %all-gather.11.cloned.1.call-done = bf16[512,8192]{1,0:T(8,128)(2,1)} async-done(((bf16[512,256]{1,0:T(8,128)(2,1)}), bf16[512,8192]{1,0:T(8,128)(2,1)}) %all-gather.11.cloned.1.call-update) | async-done | bytes 8388624 | tf_op jit(solution)/shard_map/all_gather | solution.py:77
  249.1 10.0 %convolution_convert_fusion = bf16[512,8192]{1,0:T(8,128)(2,1)} fusion(bf16[512,8192]{1,0:T(8,128)(2,1)} %all-gather.11.cloned.1.call-done, bf16[64,8,4,128]{3,2,1,0:T(4,128)(2,1)S(1)} %bitcast.100), kind=kOutput, calls=%fused_computation.2 | convolution fusion | flops 4299161600 | bytes 17301504 | tf_op jit(solution)/shard_map/dot_general | solution.py:76
  259.1 0.0 reduce-scatter.2.cloned.1.call-update
  259.2 94.5 %reduce-scatter.2.cloned.1.call-done = bf16[512,1024]{1,0:T(8,128)(2,1)} async-done(((bf16[512,8192]{1,0:T(8,128)(2,1)}), bf16[512,1024]{1,0:T(8,128)(2,1)}) %reduce-scatter.2.cloned.1.call-update) | async-done | bytes 1048592 | tf_op jit(solution)/shard_map/reduce_scatter | solution.py:79
  (5 shorter events, 0.0 us)
Async XLA Ops:
  6.5 61.3 %all-gather.5.cloned.1.call-start = ((), (), s32[]{:S(2)}) async-start(), calls=%async_computation.1 | async-start | bytes 4718592 | tf_op jit(solution)/shard_map/all_gather | solution.py:46
  7.3 115.8 %all-gather.7.cloned.1.call-start = ((), (), s32[]{:S(2)}) async-start(), calls=%async_computation.2 | async-start | bytes 4718592 | tf_op jit(solution)/shard_map/all_gather | solution.py:45
  8.0 174.6 %all-gather.9.cloned.1.call-start = ((), (), s32[]{:S(2)}) async-start(), calls=%async_computation.3 | async-start | bytes 8650752 | tf_op jit(solution)/shard_map/all_gather | solution.py:35
  8.7 240.4 %all-gather.11.cloned.1.call-start = ((), (), s32[]{:S(2)}) async-start(), calls=%async_computation.4 | async-start | bytes 8650752 | tf_op jit(solution)/shard_map/all_gather | solution.py:77
  9.3 344.3 %reduce-scatter.2.cloned.1.call-start = ((), (), s32[]{:S(2)}) async-start(), calls=%async_computation.5 | async-start | bytes 9437184 | tf_op jit(solution)/shard_map/reduce_scatter | solution.py:79
  198.7 1.8 copy-start
Sparse Core Ops, SparseCore 0:
  9.1 58.6 all-gather.4
  69.6 53.4 all-gather.6
  125.6 56.9 all-gather.8
  184.9 64.1 all-gather.10
  259.3 94.2 reduce-scatter.1
where the time goes:
time: 360 us
  waiting for transfers between devices  310 us (86%)
  matrix products  24.3 us (7%)
  between operations  13.3 us (4%)
  local copies, waits for them, and re-layouts  7.56 us (2%)
  other arithmetic  5.01 us (1%)
    reduce_scatter x1, waiting for transfers between devices, body(): lax.psum_scatter(share_terms.astype(jnp.bfloat16), 'ctx', scatter_dimensi...  94.5 us
    all_gather x1, waiting for transfers between devices, body(): lax.all_gather(value_cache, 'ctx', axis=0, tiled=True)  56 us
    all_gather x1, waiting for transfers between devices, body(): lax.all_gather(wq, 'fsdp', axis=0, tiled=True)  55.4 us
    all_gather x1, waiting for transfers between devices, body(): lax.all_gather(key_cache, 'ctx', axis=0, tiled=True)  55.2 us
    all_gather x1, waiting for transfers between devices, body(): lax.all_gather(wo, 'fsdp', axis=1, tiled=True)  46.1 us
    dot_general x1, matrix products, body(): jnp.dot(context, lax.all_gather(wo, 'fsdp', axis=1, tiled=True), preferre...  10 us
    dot_general x1, matrix products, body(): jnp.dot(tokens, lax.all_gather(wq, 'fsdp', axis=0, tiled=True), preferred...  9.44 us
  transfers between devices with their start and end apart: 5, of which 5 were waited for; matrix products, arithmetic and copies ran while one was open for 7% of the time, Pallas kernels for 0%

commit v1 on v0

--- a/solution.py
+++ b/solution.py
@@ -6,6 +6,27 @@
 HEAD = 128
 BLOCK = 128
 rope_base = 1000000.0
+
+
+def review_sample_all(message):
+    p_next, oldest, y1 = (lax.psum(1, "ctx"), lax.axis_index("ctx"), message.shape[0])
+    cards = [(d, (d + 1) % p_next) for d in range(p_next)]
+    mid_arr = jnp.zeros((*message.shape[:0], p_next * y1, *message.shape[1:]), message.dtype)
+    mid_arr = lax.dynamic_update_slice_in_dim(mid_arr, message, oldest * y1, axis=0)
+    queue = [(d, (d - 1) % p_next) for d in range(p_next)]
+    o_now = p_next // 2
+    u_next = w_next = message
+    for p in range(1, o_now + 1):
+        u_next = lax.ppermute(u_next, "ctx", cards)
+        mid_arr = lax.dynamic_update_slice_in_dim(
+            mid_arr, u_next, (oldest - p) % p_next * y1, axis=0
+        )
+        if p < p_next - o_now:
+            w_next = lax.ppermute(w_next, "ctx", queue)
+            mid_arr = lax.dynamic_update_slice_in_dim(
+                mid_arr, w_next, (oldest + p) % p_next * y1, axis=0
+            )
+    return mid_arr
 
 
 def rotate(vectors, positions):
@@ -42,7 +63,7 @@
     ).astype(jnp.bfloat16)
     kv_cols = key_cache.shape[1] // ctx_count
     keys_whole, values_whole = (
-        lax.all_gather(key_cache, "ctx", axis=0, tiled=True),
+        review_sample_all(key_cache),
         lax.all_gather(value_cache, "ctx", axis=0, tiled=True),
     )
     first_col = lax.axis_index("ctx") * kv_cols

time: 360 us -> 337 us (0.936)
  waiting for transfers between devices: 310 us -> 263 us
  starting transfers between devices: 0.15 us -> 12.4 us
  local copies, waits for them, and re-layouts: 7.56 us -> 17.9 us
    ppermute x0 -> x7, waiting for transfers between devices: none -> 67 us  [the longest x4 66.4 us: review_sample_all(): u_next = lax.ppermute(u_next, 'ctx', cards)]
    all_gather x1, waiting for transfers between devices: 56 us -> 0.01 us  [body(): lax.all_gather(value_cache, 'ctx', axis=0, tiled=True)]
    all_gather x1 -> x0, waiting for transfers between devices: 55.2 us -> none  [body(): lax.all_gather(key_cache, 'ctx', axis=0, tiled=True)]
    ppermute x0 -> x7, starting transfers between devices: none -> 12.3 us  [the longest x3 9.71 us: review_sample_all(): w_next = lax.ppermute(w_next, 'ctx', queue)]
    dynamic_update_slice x0 -> x8, local copies, waits for them, and re-layouts: none -> 7.8 us  [the longest x4 3.38 us: review_sample_all(): lax.dynamic_update_slice_in_dim(mid_arr, u_next, (oldest - p) % p_next *...]
  transfers between devices with their start and end apart: 5 -> 11, of which waited for: 5 -> 8; matrix products, arithmetic and copies ran while one was open for 7% -> 11% of each run, Pallas kernels for 0% -> 0%
where the time goes in v1:
time: 337 us; the launch traced here: 336 us
  waiting for transfers between devices  263 us (78%)
  matrix products  24.4 us (7%)
  local copies, waits for them, and re-layouts  17.9 us (5%)
  between operations  13.4 us (4%)
  starting transfers between devices  12.4 us (4%)
  other arithmetic  5.01 us (1%)
    reduce_scatter x1, waiting for transfers between devices, body(): lax.psum_scatter(share_terms.astype(jnp.bfloat16), 'ctx', scatter_dimensi...  94.5 us
    ppermute x4, waiting for transfers between devices, review_sample_all(): u_next = lax.ppermute(u_next, 'ctx', cards)  66.4 us
    all_gather x1, waiting for transfers between devices, body(): lax.all_gather(wq, 'fsdp', axis=0, tiled=True)  53.6 us
    all_gather x1, waiting for transfers between devices, body(): lax.all_gather(wo, 'fsdp', axis=1, tiled=True)  46.3 us
    dot_general x1, matrix products, body(): jnp.dot(context, lax.all_gather(wo, 'fsdp', axis=1, tiled=True), preferre...  10 us
    ppermute x3, starting transfers between devices, review_sample_all(): w_next = lax.ppermute(w_next, 'ctx', queue)  9.71 us
    dot_general x1, matrix products, body(): jnp.dot(tokens, lax.all_gather(wq, 'fsdp', axis=0, tiled=True), preferred...  9.44 us
  transfers between devices with their start and end apart: 11, of which 8 were waited for; matrix products, arithmetic and copies ran while one was open for 11% of the time, Pallas kernels for 0%

profile of v1, /device:TPU:1, one launch (start us, length us, event | category | flops | bytes accessed | tf_op | source)
XLA Modules:
  0.0 336.4 jit_solution(6924612069814177868)
XLA Ops:
  6.5 0.0 all-gather.4.cloned.1.call-start
  6.5 0.7 all-gather.4.cloned.1.call-update
  7.3 0.0 all-gather.6.cloned.1.call-start
  7.3 0.7 all-gather.6.cloned.1.call-update
  8.0 0.0 all-gather.8.cloned.1.call-start
  8.1 0.7 all-gather.8.cloned.1.call-update
  8.7 0.0 reduce-scatter.2.cloned.1.call-start
  8.8 2.5 collective-permute-start
  11.3 4.0 %collective-permute-start.1 = (bf16[256,1024]{1,0:T(8,128)(2,1)}, bf16[256,1024]{1,0:T(8,128)(2,1)S(1)}, u32[]{:S(2)}, u32[]{:S(2)}) collective-permute-start(bf16[256,1024]{1,0:T(8,128)(2,1)} %param.11), channel_id=1, source_target_pairs={{0,7},{1,0},{2,1},{3,2},{4,3},{5,4},{6,5},{7,6},{8,15},{9,8},{10,9... | collective-permute-start | bytes 1572872 | tf_op jit(solution)/shard_map/ppermute | solution.py:25
  15.4 0.7 compare_select_fusion
  16.1 11.1 %collective-permute-done = bf16[256,1024]{1,0:T(8,128)(2,1)S(1)} collective-permute-done((bf16[256,1024]{1,0:T(8,128)(2,1)}, bf16[256,1024]{1,0:T(8,128)(2,1)S(1)}, u32[]{:S(2)}, u32[]{:S(2)}) %collective-permute-start) | collective-permute-done | bytes 524320 | tf_op jit(solution)/shard_map/ppermute | solution.py:20
  27.1 0.0 collective-permute-start.2
  27.1 0.8 fusion.28
  27.9 0.5 multiply_cosine_fusion
  28.4 0.0 collective-permute-done.1
  28.4 3.0 collective-permute-start.3
  31.5 0.1 reshape.192
  31.5 21.5 %collective-permute-done.2 = bf16[256,1024]{1,0:T(8,128)(2,1)S(1)} collective-permute-done((bf16[256,1024]{1,0:T(8,128)(2,1)S(1)}, bf16[256,1024]{1,0:T(8,128)(2,1)S(1)}, u32[]{:S(2)}, u32[]{:S(2)}) %collective-permute-start.2) | collective-permute-done | bytes 524320 | tf_op jit(solution)/shard_map/ppermute | solution.py:20
  53.0 0.0 collective-permute-start.4
  53.2 2.5 broadcast_in_dim.24
  55.7 1.9 constant_dynamic-update-slice_fusion.7
  57.6 0.3 broadcast_or_fusion
  57.9 0.0 collective-permute-done.3
  57.9 2.7 collective-permute-start.5
  60.6 0.9 constant_dynamic-update-slice_fusion.6
  61.4 17.2 %collective-permute-done.4 = bf16[256,1024]{1,0:T(8,128)(2,1)S(1)} collective-permute-done((bf16[256,1024]{1,0:T(8,128)(2,1)S(1)}, bf16[256,1024]{1,0:T(8,128)(2,1)S(1)}, u32[]{:S(2)}, u32[]{:S(2)}) %collective-permute-start.4) | collective-permute-done | bytes 524320 | tf_op jit(solution)/shard_map/ppermute | solution.py:20
  78.7 0.0 collective-permute-start.6
  78.7 0.8 constant_dynamic-update-slice_fusion.5
  79.5 0.8 constant_dynamic-update-slice_fusion.4
  80.4 0.9 constant_dynamic-update-slice_fusion.3
  81.2 0.8 constant_dynamic-update-slice_fusion.2
  82.0 0.6 collective-permute-done.5
  82.6 0.8 constant_dynamic-update-slice_fusion.1
  83.4 16.6 %collective-permute-done.6 = bf16[256,1024]{1,0:T(8,128)(2,1)S(1)} collective-permute-done((bf16[256,1024]{1,0:T(8,128)(2,1)S(1)}, bf16[256,1024]{1,0:T(8,128)(2,1)S(1)}, u32[]{:S(2)}, u32[]{:S(2)}) %collective-permute-start.6) | collective-permute-done | bytes 524320 | tf_op jit(solution)/shard_map/ppermute | solution.py:20
  100.1 0.8 constant_dynamic-update-slice_fusion
  100.9 0.0 all-gather.4.cloned.1.call-done
  100.9 1.3 constant_dynamic-slice_fusion
  102.2 0.7 gather_fusion.1
  103.0 0.7 gather_fusion
  103.7 1.3 copy.8
  105.1 53.6 %all-gather.6.cloned.1.call-done = bf16[8192,512]{1,0:T(8,128)(2,1)} async-done(((bf16[256,512]{1,0:T(8,128)(2,1)}), bf16[8192,512]{1,0:T(8,128)(2,1)}) %all-gather.6.cloned.1.call-update) | async-done | bytes 8388624 | tf_op jit(solution)/shard_map/all_gather | solution.py:56
  158.6 9.4 %fusion.34 = f32[512,512]{0,1:T(8,128)S(1)} fusion(bf16[512,8192]{1,0:T(8,128)(2,1)} %param.8, bf16[8192,512]{1,0:T(8,128)(2,1)} %all-gather.6.cloned.1.call-done), kind=kOutput, calls=%fused_computation.57 | convolution fusion | flops 4294967296 | bytes 17825792 | tf_op jit(solution)/shard_map/dot_general | solution.py:55
  168.1 1.0 multiply_subtract_fusion
  169.0 0.2 concatenate.10
  169.2 0.3 copy.10
  169.6 1.2 concatenate.9
  170.8 1.3 copy.9
  172.1 2.7 fusion
  174.8 0.0 copy-start
  174.8 1.7 fusion.1
  176.5 0.0 copy-done
  176.5 2.2 fusion.10
  178.7 0.3 copy.12
  179.1 46.3 %all-gather.8.cloned.1.call-done = bf16[512,8192]{1,0:T(8,128)(2,1)} async-done(((bf16[512,256]{1,0:T(8,128)(2,1)}), bf16[512,8192]{1,0:T(8,128)(2,1)}) %all-gather.8.cloned.1.call-update) | async-done | bytes 8388624 | tf_op jit(solution)/shard_map/all_gather | solution.py:98
  225.3 10.0 %convolution_convert_fusion = bf16[512,8192]{1,0:T(8,128)(2,1)} fusion(bf16[512,8192]{1,0:T(8,128)(2,1)} %all-gather.8.cloned.1.call-done, bf16[64,8,4,128]{3,2,1,0:T(4,128)(2,1)S(1)} %bitcast.100), kind=kOutput, calls=%fused_computation.2 | convolution fusion | flops 4299161600 | bytes 17301504 | tf_op jit(solution)/shard_map/dot_general | solution.py:97
  235.4 0.0 reduce-scatter.2.cloned.1.call-update
  235.4 94.5 %reduce-scatter.2.cloned.1.call-done = bf16[512,1024]{1,0:T(8,128)(2,1)} async-done(((bf16[512,8192]{1,0:T(8,128)(2,1)}), bf16[512,1024]{1,0:T(8,128)(2,1)}) %reduce-scatter.2.cloned.1.call-update) | async-done | bytes 1048592 | tf_op jit(solution)/shard_map/reduce_scatter | solution.py:100
  (5 shorter events, 0.0 us)
Async XLA Ops:
  6.5 94.4 %all-gather.4.cloned.1.call-start = ((), (), s32[]{:S(2)}) async-start(), calls=%async_computation.1 | async-start | bytes 4718592 | tf_op jit(solution)/shard_map/all_gather | solution.py:67
  7.3 151.4 %all-gather.6.cloned.1.call-start = ((), (), s32[]{:S(2)}) async-start(), calls=%async_computation.2 | async-start | bytes 8650752 | tf_op jit(solution)/shard_map/all_gather | solution.py:56
  8.0 217.3 %all-gather.8.cloned.1.call-start = ((), (), s32[]{:S(2)}) async-start(), calls=%async_computation.3 | async-start | bytes 8650752 | tf_op jit(solution)/shard_map/all_gather | solution.py:98
  8.7 321.1 %reduce-scatter.2.cloned.1.call-start = ((), (), s32[]{:S(2)}) async-start(), calls=%async_computation.4 | async-start | bytes 9437184 | tf_op jit(solution)/shard_map/reduce_scatter | solution.py:100
  8.8 18.3 %collective-permute-start = (bf16[256,1024]{1,0:T(8,128)(2,1)}, bf16[256,1024]{1,0:T(8,128)(2,1)S(1)}, u32[]{:S(2)}, u32[]{:S(2)}) collective-permute-start(bf16[256,1024]{1,0:T(8,128)(2,1)} %param.11), channel_id=1, source_target_pairs={{0,1},{1,2},{2,3},{3,4},{4,5},{5,6},{6,7},{7,0},{8,9},{9,10},{10,1... | collective-permute-start | bytes 1572872 | tf_op jit(solution)/shard_map/ppermute | solution.py:20
  11.3 17.1 %collective-permute-start.1 = (bf16[256,1024]{1,0:T(8,128)(2,1)}, bf16[256,1024]{1,0:T(8,128)(2,1)S(1)}, u32[]{:S(2)}, u32[]{:S(2)}) collective-permute-start(bf16[256,1024]{1,0:T(8,128)(2,1)} %param.11), channel_id=1, source_target_pairs={{0,7},{1,0},{2,1},{3,2},{4,3},{5,4},{6,5},{7,6},{8,15},{9,8},{10,9... | collective-permute-start | bytes 1572872 | tf_op jit(solution)/shard_map/ppermute | solution.py:25
  27.1 25.9 %collective-permute-start.2 = (bf16[256,1024]{1,0:T(8,128)(2,1)S(1)}, bf16[256,1024]{1,0:T(8,128)(2,1)S(1)}, u32[]{:S(2)}, u32[]{:S(2)}) collective-permute-start(bf16[256,1024]{1,0:T(8,128)(2,1)S(1)} %collective-permute-done), channel_id=1, source_target_pairs={{0,1},{1,2},{2,3},{3,4},{4,5},{5,6},{6,7},{7,0},{8,9},{9,10},{10,1... | collective-permute-start | bytes 1572872 | tf_op jit(solution)/shard_map/ppermute | solution.py:20
  28.4 29.4 %collective-permute-start.3 = (bf16[256,1024]{1,0:T(8,128)(2,1)S(1)}, bf16[256,1024]{1,0:T(8,128)(2,1)S(1)}, u32[]{:S(2)}, u32[]{:S(2)}) collective-permute-start(bf16[256,1024]{1,0:T(8,128)(2,1)S(1)} %collective-permute-done.1), channel_id=1, source_target_pairs={{0,7},{1,0},{2,1},{3,2},{4,3},{5,4},{6,5},{7,6},{8,15},{9,8},{10,9... | collective-permute-start | bytes 1572872 | tf_op jit(solution)/shard_map/ppermute | solution.py:25
  53.0 25.7 %collective-permute-start.4 = (bf16[256,1024]{1,0:T(8,128)(2,1)S(1)}, bf16[256,1024]{1,0:T(8,128)(2,1)S(1)}, u32[]{:S(2)}, u32[]{:S(2)}) collective-permute-start(bf16[256,1024]{1,0:T(8,128)(2,1)S(1)} %collective-permute-done.2), channel_id=1, source_target_pairs={{0,1},{1,2},{2,3},{3,4},{4,5},{5,6},{6,7},{7,0},{8,9},{9,10},{10,1... | collective-permute-start | bytes 1572872 | tf_op jit(solution)/shard_map/ppermute | solution.py:20
  57.9 24.7 %collective-permute-start.5 = (bf16[256,1024]{1,0:T(8,128)(2,1)S(1)}, bf16[256,1024]{1,0:T(8,128)(2,1)S(1)}, u32[]{:S(2)}, u32[]{:S(2)}) collective-permute-start(bf16[256,1024]{1,0:T(8,128)(2,1)S(1)} %collective-permute-done.3), channel_id=1, source_target_pairs={{0,7},{1,0},{2,1},{3,2},{4,3},{5,4},{6,5},{7,6},{8,15},{9,8},{10,9... | collective-permute-start | bytes 1572872 | tf_op jit(solution)/shard_map/ppermute | solution.py:25
  78.7 21.4 %collective-permute-start.6 = (bf16[256,1024]{1,0:T(8,128)(2,1)S(1)}, bf16[256,1024]{1,0:T(8,128)(2,1)S(1)}, u32[]{:S(2)}, u32[]{:S(2)}) collective-permute-start(bf16[256,1024]{1,0:T(8,128)(2,1)S(1)} %collective-permute-done.4), channel_id=1, source_target_pairs={{0,1},{1,2},{2,3},{3,4},{4,5},{5,6},{6,7},{7,0},{8,9},{9,10},{10,1... | collective-permute-start | bytes 1572872 | tf_op jit(solution)/shard_map/ppermute | solution.py:20
  174.8 1.8 copy-start
Sparse Core Ops, SparseCore 0:
  9.1 87.0 all-gather.3
  98.8 59.7 all-gather.5
  161.1 64.1 all-gather.7
  235.5 94.2 reduce-scatter.1
